TPU v7x, 128 devices: a whole 4x4x4 slice. The times are simulated.
128 devices in a mesh: rep: 16 (over x_lo, z, core), shard: 8 (over x_hi, y).
Axes of the slice: x: 4 (x_hi: 2, x_lo: 2; x = x_hi * 2 + x_lo), y: 4, z: 4, core: 2. Of those that a mesh axis runs over, the one named last changes fastest.
Arguments:
- latents: bfloat16 [16, 1024, 1024], P('rep', 'shard'), may hold values from -6 to 6
- cond: bfloat16 [16, 1024], P('rep'), may hold values from -6 to 6
- cotangent: bfloat16 [16, 1024, 1024], P('rep', 'shard'), may hold values from -6 to 6
- w_qkv: bfloat16 [1024, 3072], P('shard'), may hold values from -0.1875 to 0.1875
- bias_qv: bfloat16 [2048], P('shard'), may hold values from -3 to 3
- w_proj: bfloat16 [1024, 1024], P('shard'), may hold values from -1 to 1
- b_proj: bfloat16 [1024], P('shard'), may hold values from -3 to 3
- w_fc1: bfloat16 [1024, 4096], P('shard'), may hold values from -0.1875 to 0.1875
- b_fc1: bfloat16 [4096], P('shard'), may hold values from -3 to 3
- w_fc2: bfloat16 [4096, 1024], P('shard'), may hold values from -0.09375 to 0.09375
- b_fc2: bfloat16 [1024], P('shard'), may hold values from -3 to 3
- w_ada: bfloat16 [1024, 6144], P('shard'), may hold values from -0.1875 to 0.1875
- b_ada: bfloat16 [6144], P('shard'), may hold values from -3 to 3
Outputs:
- output: bfloat16 [16, 1024, 1024], P('rep', 'shard')
- grad_latents: bfloat16 [16, 1024, 1024], P('rep', 'shard')
- grad_cond: float32 [16, 1024], P('rep')
- grad_w_qkv: float32 [1024, 3072], P('shard')
- grad_bias_qv: float32 [2048], P('shard')
- grad_w_proj: float32 [1024, 1024], P('shard')
- grad_b_proj: float32 [1024], P('shard')
- grad_w_fc1: float32 [1024, 4096], P('shard')
- grad_b_fc1: float32 [4096], P('shard')
- grad_w_fc2: float32 [4096, 1024], P('shard')
- grad_b_fc2: float32 [1024], P('shard')
- grad_w_ada: float32 [1024, 6144], P('shard')
- grad_b_ada: float32 [6144], P('shard')
All inputs are finite; a program needn't handle non-finite values.
Results may differ from a plain program's by a relative error of at most 0.025.
Values may be sent and summed in bfloat16 or wider, within the bound.
No kernel may reach another device: no remote copies, remote signals or barrier semaphores. Data moves between devices by JAX's collectives and lax.ppermute only.
A program may use at most 192 MiB of HBM per device.

v0:
```python
import jax
import jax.numpy as jnp
from jax import lax
from jax.sharding import PartitionSpec as P

HEAD = 64
epsilon = 1e-06
highest = lax.Precision.HIGHEST


def as_sent(value):
    return jax.tree.map(lambda a: a.astype(jnp.bfloat16) if a.dtype == jnp.float32 else a, value)


def layer_norm(values):
    centered = values - jnp.mean(values, axis=-1, keepdims=True)
    variance = jnp.mean(centered * centered, axis=-1, keepdims=True)
    return centered * lax.rsqrt(variance + epsilon)


def sigmoid_linear(values):
    return values / (1.0 + jnp.exp(-values))


def gelu_tanh(values):
    return (
        0.5
        * values
        * (1.0 + jnp.tanh(0.7978845608028654 * (values + 0.044715 * values * values * values)))
    )


def project(left, right):
    return jnp.einsum("lrd,de->lre", left, right, preferred_element_type=jnp.float32)


def project_back(left, right):
    return jnp.einsum("lre,de->lrd", left, right, preferred_element_type=jnp.float32)


def on_device(
    latents,
    cond,
    cotangent,
    w_qkv,
    bias_qv,
    w_proj,
    b_proj,
    w_fc1,
    b_fc1,
    w_fc2,
    b_fc2,
    w_ada,
    b_ada,
):
    count_lat = latents.shape[0]
    rows = latents.shape[1]
    features = latents.shape[2]
    heads = features // HEAD
    score_scale = HEAD ** (-0.5)
    gathered = (
        lax.all_gather(w_qkv, "shard", axis=0, tiled=True),
        lax.all_gather(bias_qv, "shard", axis=0, tiled=True),
        lax.all_gather(w_proj, "shard", axis=0, tiled=True),
        lax.all_gather(b_proj, "shard", axis=0, tiled=True),
        lax.all_gather(w_fc1, "shard", axis=0, tiled=True),
        lax.all_gather(b_fc1, "shard", axis=0, tiled=True),
        lax.all_gather(w_fc2, "shard", axis=0, tiled=True),
        lax.all_gather(b_fc2, "shard", axis=0, tiled=True),
        lax.all_gather(w_ada, "shard", axis=0, tiled=True),
        lax.all_gather(b_ada, "shard", axis=0, tiled=True),
    )
    whole_qkv = gathered[0]
    whole_proj = gathered[2]
    whole_fc1 = gathered[4]
    whole_fc2 = gathered[6]
    whole_ada = gathered[8]
    bias_wide = gathered[1].astype(jnp.float32)
    stream = latents.astype(jnp.float32)
    cond_value = cond.astype(jnp.float32)
    cond_silu, silu_pull = jax.vjp(sigmoid_linear, cond_value)
    cond_low = cond_silu.astype(jnp.bfloat16)
    modulation = jnp.dot(cond_low, whole_ada, preferred_element_type=jnp.float32) + gathered[
        9
    ].astype(jnp.float32)
    shift_first, scale_first, gate_first, shift_second, scale_second, gate_second = jnp.split(
        modulation[:, None, :], 6, axis=2
    )
    norm_first, first_pull = jax.vjp(layer_norm, stream)
    attend_in = (norm_first * (1.0 + scale_first) + shift_first).astype(jnp.bfloat16)
    packed = project(attend_in, whole_qkv)
    queries = (packed[:, :, :features] + bias_wide[:features]).astype(jnp.bfloat16)
    keyset = packed[:, :, features : 2 * features].astype(jnp.bfloat16)
    valueset = (packed[:, :, 2 * features :] + bias_wide[features:]).astype(jnp.bfloat16)
    key_all, value_all = (
        lax.all_gather(keyset, "shard", axis=1, tiled=True),
        lax.all_gather(valueset, "shard", axis=1, tiled=True),
    )
    length = key_all.shape[1]
    query_heads = queries.reshape(count_lat, rows, heads, HEAD)
    key_heads = key_all.reshape(count_lat, length, heads, HEAD)
    value_heads = value_all.reshape(count_lat, length, heads, HEAD)
    scores = (
        jnp.einsum("lqhe,lkhe->lhqk", query_heads, key_heads, preferred_element_type=jnp.float32)
        * score_scale
    )
    row_peak = jnp.max(scores, axis=-1, keepdims=True)
    powered = jnp.exp(scores - row_peak)
    row_total = jnp.sum(powered, axis=-1, keepdims=True)
    attention = powered / row_total
    log_total = row_peak + jnp.log(row_total)
    mixed_heads = jnp.einsum(
        "lhqk,lkhe->lqhe",
        attention.astype(jnp.bfloat16),
        value_heads,
        preferred_element_type=jnp.float32,
    )
    mixed_low = mixed_heads.reshape(count_lat, rows, features).astype(jnp.bfloat16)
    branch = project(mixed_low, whole_proj) + gathered[3].astype(jnp.float32)
    middle = stream + gate_first * branch
    norm_second, second_pull = jax.vjp(layer_norm, middle)
    feed_in = (norm_second * (1.0 + scale_second) + shift_second).astype(jnp.bfloat16)
    hidden = project(feed_in, whole_fc1) + gathered[5].astype(jnp.float32)
    active_value, gelu_pull = jax.vjp(gelu_tanh, hidden)
    active_low = active_value.astype(jnp.bfloat16)
    branch_second = project(active_low, whole_fc2) + gathered[7].astype(jnp.float32)
    output = (middle + gate_second * branch_second).astype(jnp.bfloat16)
    regathered = (
        lax.all_gather(w_qkv, "shard", axis=0, tiled=True),
        lax.all_gather(w_proj, "shard", axis=0, tiled=True),
        lax.all_gather(w_fc1, "shard", axis=0, tiled=True),
        lax.all_gather(w_fc2, "shard", axis=0, tiled=True),
        lax.all_gather(w_ada, "shard", axis=0, tiled=True),
    )
    back_qkv = regathered[0]
    back_proj = regathered[1]
    back_fc1 = regathered[2]
    back_fc2 = regathered[3]
    back_ada = regathered[4]
    upstream = cotangent.astype(jnp.float32)
    grad_gate_second = jnp.sum(upstream * branch_second, axis=1)
    grad_branch_second = (upstream * gate_second).astype(jnp.bfloat16)
    grad_active = project_back(grad_branch_second, back_fc2)
    grad_hidden = gelu_pull(grad_active)[0].astype(jnp.bfloat16)
    grad_feed = project_back(grad_hidden, back_fc1)
    grad_scale_second = jnp.sum(grad_feed * norm_second, axis=1)
    grad_shift_second = jnp.sum(grad_feed, axis=1)
    grad_middle = upstream + second_pull(grad_feed * (1.0 + scale_second))[0]
    grad_gate_first = jnp.sum(grad_middle * branch, axis=1)
    grad_branch = (grad_middle * gate_first).astype(jnp.bfloat16)
    grad_mixed = (
        project_back(grad_branch, back_proj)
        .astype(jnp.bfloat16)
        .reshape(count_lat, rows, heads, HEAD)
    )
    again_scores = (
        jnp.einsum("lqhe,lkhe->lhqk", query_heads, key_heads, preferred_element_type=jnp.float32)
        * score_scale
    )
    again_probs = jnp.exp(again_scores - log_total)
    grad_probs = jnp.einsum(
        "lqhe,lkhe->lhqk", grad_mixed, value_heads, preferred_element_type=jnp.float32
    )
    grad_value = jnp.einsum(
        "lhqk,lqhe->lkhe",
        again_probs.astype(jnp.bfloat16),
        grad_mixed,
        preferred_element_type=jnp.float32,
    )
    row_delta = jnp.sum(again_probs * grad_probs, axis=-1, keepdims=True)
    grad_scores = (again_probs * (grad_probs - row_delta)).astype(jnp.bfloat16)
    grad_query = (
        (
            jnp.einsum(
                "lhqk,lkhe->lqhe", grad_scores, key_heads, preferred_element_type=jnp.float32
            )
            * score_scale
        )
        .reshape(count_lat, rows, features)
        .astype(jnp.bfloat16)
    )
    grad_key = (
        jnp.einsum("lhqk,lqhe->lkhe", grad_scores, query_heads, preferred_element_type=jnp.float32)
        * score_scale
    )
    key_owned, value_owned = (
        lax.psum_scatter(
            grad_key.reshape(count_lat, length, features).astype(jnp.bfloat16),
            "shard",
            scatter_dimension=1,
            tiled=True,
        ).astype(jnp.float32),
        lax.psum_scatter(
            grad_value.reshape(count_lat, length, features).astype(jnp.bfloat16),
            "shard",
            scatter_dimension=1,
            tiled=True,
        ).astype(jnp.float32),
    )
    key_low = key_owned.astype(jnp.bfloat16)
    value_low = value_owned.astype(jnp.bfloat16)
    grad_packed = jnp.concatenate([grad_query, key_low, value_low], axis=2)
    grad_attend = project_back(grad_packed, back_qkv)
    grad_scale_first = jnp.sum(grad_attend * norm_first, axis=1)
    grad_shift_first = jnp.sum(grad_attend, axis=1)
    grad_stream = grad_middle + first_pull(grad_attend * (1.0 + scale_first))[0]
    grad_latents = grad_stream.astype(jnp.bfloat16)
    grad_modulation = jnp.concatenate(
        [
            grad_shift_first,
            grad_scale_first,
            grad_gate_first,
            grad_shift_second,
            grad_scale_second,
            grad_gate_second,
        ],
        axis=1,
    )
    cond_wide = cond_low.astype(jnp.float32)
    cond_term = jnp.einsum(
        "lm,dm->ld",
        grad_modulation,
        back_ada,
        precision=highest,
        preferred_element_type=jnp.float32,
    )
    cond_total = lax.psum(cond_term, "shard")
    grad_cond = silu_pull(cond_total)[0]
    term_qkv = jnp.einsum("lrc,lre->ce", attend_in, grad_packed, preferred_element_type=jnp.float32)
    term_proj = jnp.einsum(
        "lrc,lre->ce", mixed_low, grad_branch, preferred_element_type=jnp.float32
    )
    term_fc1 = jnp.einsum("lrc,lre->ce", feed_in, grad_hidden, preferred_element_type=jnp.float32)
    pieces = [term_qkv, term_proj, term_fc1]
    pieces.append(jnp.dot(cond_wide.T, grad_modulation, precision=highest))
    row_owned = lax.psum_scatter(
        jnp.concatenate(pieces, axis=1).astype(jnp.bfloat16),
        "shard",
        scatter_dimension=0,
        tiled=True,
    ).astype(jnp.float32)
    units = active_low.shape[2]
    second_owned = lax.psum_scatter(
        jnp.einsum(
            "lrc,lre->ce", active_low, grad_branch_second, preferred_element_type=jnp.float32
        ).astype(jnp.bfloat16),
        "shard",
        scatter_dimension=0,
        tiled=True,
    )
    bias_query = jnp.sum(grad_query.astype(jnp.float32), axis=(0, 1))
    bias_value = jnp.sum(value_low.astype(jnp.float32), axis=(0, 1))
    base_terms = (
        jnp.concatenate([bias_query, bias_value], axis=0),
        jnp.sum(grad_branch.astype(jnp.float32), axis=(0, 1)),
        jnp.sum(grad_hidden.astype(jnp.float32), axis=(0, 1)),
        jnp.sum(grad_branch_second.astype(jnp.float32), axis=(0, 1)),
    )
    bias_terms = base_terms + (jnp.sum(grad_modulation, axis=0),)
    bias_owned = jax.tree.map(
        lambda part: part.astype(jnp.float32),
        lax.psum_scatter(as_sent(bias_terms), "shard", scatter_dimension=0, tiled=True),
    )
    wide_qkv = 3 * features
    owned_qkv = row_owned[:, :wide_qkv]
    owned_proj = row_owned[:, wide_qkv : wide_qkv + features]
    owned_fc1 = row_owned[:, wide_qkv + features : wide_qkv + features + units]
    owned_ada = row_owned[:, wide_qkv + features + units :]
    owned_ada_bias = bias_owned[4]
    totals = (
        lax.psum(owned_qkv.astype(jnp.bfloat16), "rep").astype(jnp.float32),
        lax.psum(bias_owned[0].astype(jnp.bfloat16), "rep").astype(jnp.float32),
        lax.psum(owned_proj.astype(jnp.bfloat16), "rep").astype(jnp.float32),
        lax.psum(bias_owned[1].astype(jnp.bfloat16), "rep").astype(jnp.float32),
        lax.psum(owned_fc1.astype(jnp.bfloat16), "rep").astype(jnp.float32),
        lax.psum(bias_owned[2].astype(jnp.bfloat16), "rep").astype(jnp.float32),
        lax.psum(second_owned, "rep").astype(jnp.float32),
        lax.psum(bias_owned[3].astype(jnp.bfloat16), "rep").astype(jnp.float32),
        lax.psum(owned_ada.astype(jnp.bfloat16), "rep").astype(jnp.float32),
        lax.psum(owned_ada_bias.astype(jnp.bfloat16), "rep").astype(jnp.float32),
    )
    return (
        output,
        grad_latents,
        grad_cond,
        totals[0],
        totals[1],
        totals[2],
        totals[3],
        totals[4],
        totals[5],
        totals[6],
        totals[7],
        totals[8],
        totals[9],
    )


def solution(mesh):
    placed = (
        P("rep", "shard", None),
        P("rep", None),
        P("rep", "shard", None),
        P("shard", None),
        P("shard"),
        P("shard", None),
        P("shard"),
        P("shard", None),
        P("shard"),
        P("shard", None),
        P("shard"),
        P("shard", None),
        P("shard"),
    )
    return jax.shard_map(
        on_device,
        mesh=mesh,
        in_specs=placed,
        out_specs=(
            P("rep", "shard", None),
            P("rep", "shard", None),
            P("rep", None),
            P("shard", None),
            P("shard"),
            P("shard", None),
            P("shard"),
            P("shard", None),
            P("shard"),
            P("shard", None),
            P("shard"),
            P("shard", None),
            P("shard"),
        ),
        check_vma=False,
    )
```

profile of v0, /device:TPU:0, one launch (start us, length us, event | category | flops | bytes accessed | tf_op | source)
XLA Modules:
  0.0 1435.8 jit_solution(15415909941565255366)
XLA Ops:
  10.1 34.8 %all-gather = bf16[8,1,768]{2,1,0:T(2,128)(2,1)S(1)} all-gather(bf16[1,1,768]{2,1,0:T(2,128)(2,1)S(1)} %reshape.411), channel_id=1, replica_groups=mesh['rep'=16,'shard'=8] {'shard'}, dimensions={0}, use_global_device_ids=true | all-gather | bytes 13824 | tf_op jit(solution)/shard_map/all_gather | solution.py:71
  44.8 22.8 %all-gather.1 = bf16[8,1,256]{2,1,0:T(2,128)(2,1)S(1)} all-gather(bf16[1,1,256]{2,1,0:T(2,128)(2,1)S(1)} %reshape.413), channel_id=1, replica_groups=mesh['rep'=16,'shard'=8] {'shard'}, dimensions={0}, use_global_device_ids=true | all-gather | bytes 4608 | tf_op jit(solution)/shard_map/all_gather | solution.py:63
  70.0 87.9 %all-gather.13.cloned.1.call-done = bf16[1024,6144]{1,0:T(8,128)(2,1)} async-done(((bf16[128,6144]{1,0:T(8,128)(2,1)}), bf16[1024,6144]{1,0:T(8,128)(2,1)}) %all-gather.13.cloned.1.call-update) | async-done | bytes 12582928 | tf_op jit(solution)/shard_map/all_gather | solution.py:70
  157.9 6.3 fusion.53
  164.2 82.7 %all-gather.15.cloned.1.call-done = bf16[1024,3072]{1,0:T(8,128)(2,1)} async-done(((bf16[128,3072]{1,0:T(8,128)(2,1)}), bf16[1024,3072]{1,0:T(8,128)(2,1)}) %all-gather.15.cloned.1.call-update) | async-done | bytes 6291472 | tf_op jit(solution)/shard_map/all_gather | solution.py:62
  246.9 3.9 convolution_bitcast_fusion
  254.4 18.8 %all-gather.2 = bf16[8,1,128]{2,1,0:T(2,128)(2,1)S(1)} all-gather(bf16[1,1,128]{2,1,0:T(2,128)(2,1)S(1)} %bitcast.211), channel_id=1, replica_groups=mesh['rep'=16,'shard'=8] {'shard'}, dimensions={0}, use_global_device_ids=true | all-gather | bytes 2304 | tf_op jit(solution)/shard_map/all_gather | solution.py:65
  273.3 29.7 %all-gather.3 = bf16[8,1,512]{2,1,0:T(2,128)(2,1)S(1)} all-gather(bf16[1,1,512]{2,1,0:T(2,128)(2,1)S(1)} %reshape.417), channel_id=1, replica_groups=mesh['rep'=16,'shard'=8] {'shard'}, dimensions={0}, use_global_device_ids=true | all-gather | bytes 9216 | tf_op jit(solution)/shard_map/all_gather | solution.py:67
  303.8 3.9 copy.40
  307.7 50.6 %all-gather.19.cloned.1.call-done = bf16[1,1024,1024]{2,1,0:T(8,128)(2,1)} async-done(((bf16[1,128,1024]{2,1,0:T(8,128)(2,1)}), bf16[1,1024,1024]{2,1,0:T(8,128)(2,1)}) %all-gather.19.cloned.1.call-update) | async-done | bytes 2097168 | tf_op jit(solution)/shard_map/all_gather | solution.py:96
  358.3 2.9 copy.42
  366.1 2.9 fusion.16
  369.0 43.3 %all-gather.21.cloned.1.call-done = bf16[1024,1024]{1,0:T(8,128)(2,1)} async-done(((bf16[128,1024]{1,0:T(8,128)(2,1)}), bf16[1024,1024]{1,0:T(8,128)(2,1)}) %all-gather.21.cloned.1.call-update) | async-done | bytes 2097168 | tf_op jit(solution)/shard_map/all_gather | solution.py:64
  412.3 2.9 fusion.70
  415.5 104.0 %all-gather.23.cloned.1.call-done = bf16[1024,4096]{1,0:T(8,128)(2,1)} async-done(((bf16[128,4096]{1,0:T(8,128)(2,1)}), bf16[1024,4096]{1,0:T(8,128)(2,1)}) %all-gather.23.cloned.1.call-update) | async-done | bytes 8388624 | tf_op jit(solution)/shard_map/all_gather | solution.py:66
  519.5 6.1 convolution_add_fusion
  525.6 101.2 %all-gather.25.cloned.1.call-done = bf16[4096,1024]{1,0:T(8,128)(2,1)} async-done(((bf16[512,1024]{1,0:T(8,128)(2,1)}), bf16[4096,1024]{1,0:T(8,128)(2,1)}) %all-gather.25.cloned.1.call-update) | async-done | bytes 8388624 | tf_op jit(solution)/shard_map/all_gather | solution.py:68
  626.8 8.3 fusion.74
  635.1 3.0 fusion.33
  643.4 6.7 fusion.13
  650.1 10.9 copy.47
  661.0 4.3 copy.54
  665.5 6.8 multiply_reduce_fusion
  672.4 4.6 multiply_convert_fusion.1
  681.0 11.0 copy.45
  691.9 4.4 copy.55
  696.4 18.8 %all-gather.4 = bf16[8,1,128]{2,1,0:T(2,128)(2,1)S(1)} all-gather(bf16[1,1,128]{2,1,0:T(2,128)(2,1)S(1)} %bitcast.212), channel_id=1, replica_groups=mesh['rep'=16,'shard'=8] {'shard'}, dimensions={0}, use_global_device_ids=true | all-gather | bytes 2304 | tf_op jit(solution)/shard_map/all_gather | solution.py:69
  715.3 3.1 convolution_convert_fusion.3
  718.4 3.9 copy.44
  722.3 4.1 fusion.73
  726.4 5.7 convolution_convert_fusion.1
  732.1 6.2 reduce-scatter.15.cloned.1.call-done
  740.3 76.1 %reduce-scatter.13.cloned.1.call-done = bf16[128,1024]{1,0:T(8,128)(2,1)} async-done(((bf16[1024,1024]{1,0:T(8,128)(2,1)}), bf16[128,1024]{1,0:T(8,128)(2,1)}) %reduce-scatter.13.cloned.1.call-update) | async-done | bytes 262160
  819.0 4.6 convolution_convert_fusion.2
  823.6 6.2 fusion.28
  832.2 6.2 fusion.30
  838.5 7.5 multiply_convert_fusion
  846.0 19.0 %pad_maximum_fusion = bf16[1024,14336]{1,0:T(8,128)(2,1)} fusion(bf16[1024,6144]{1,0:T(8,128)(2,1)} %multiply_convert_fusion, bf16[1024,4096]{1,0:T(8,128)(2,1)} %convolution_convert_fusion.1, bf16[1024,1024]{1,0:T(8,128)(2,1)S(1)} %copy-done.5, bf16[1024,3072]{1,0:T(8,128)(2,1)} %convolution_convert_fusion.2), kind=kLoop, calls=%fused_computation | loop fusion | flops 117440512 | bytes 58720256 | tf_op jit(solution)/shard_map/concatenate | solution.py:237
  866.0 5.6 convolution_convert_fusion
  871.6 294.5 %reduce-scatter.9.cloned.1.call-done = bf16[128,14336]{1,0:T(8,128)(2,1)} async-done(((bf16[1024,14336]{1,0:T(8,128)(2,1)}), bf16[128,14336]{1,0:T(8,128)(2,1)}) %reduce-scatter.9.cloned.1.call-update) | async-done | bytes 3670032 | tf_op jit(solution)/shard_map/reduce_scatter | solution.py:236
  1172.2 2.7 slice.51
  1174.9 108.2 %reduce-scatter.11.cloned.1.call-done = bf16[512,1024]{1,0:T(8,128)(2,1)} async-done(((bf16[4096,1024]{1,0:T(8,128)(2,1)}), bf16[512,1024]{1,0:T(8,128)(2,1)}) %reduce-scatter.11.cloned.1.call-update) | async-done | bytes 1048592 | tf_op jit(solution)/shard_map/reduce_scatter | solution.py:243
  1286.4 38.0 %all-reduce.7 = (bf16[2048]{0:T(1024)(128)(2,1)S(1)}, bf16[1024]{0:T(1024)(128)(2,1)S(1)}, bf16[4096]{0:T(1024)(128)(2,1)S(1)}, bf16[1024]{0:T(1024)(128)(2,1)S(1)}, bf16[6144]{0:T(1024)(128)(2,1)S(1)}) all-reduce(bf16[2048]{0:T(1024)(128)(2,1)S(1)} %pad_maximum_fusion.1, ...), channel_id=5, replica_groups=mesh['rep'=16,'shard'=8] {'shard'}, use_global_device_ids=true, to_apply=%region_24.0.clone | all-reduce | flops 14336 | bytes 57344
  1324.8 27.9 %all-reduce.5 = (bf16[256]{0:T(256)(128)(2,1)S(1)}, bf16[128]{0:T(256)(128)(2,1)S(1)}, bf16[512]{0:T(512)(128)(2,1)S(1)}, bf16[128]{0:T(256)(128)(2,1)S(1)}, bf16[768]{0:T(1024)(128)(2,1)S(1)}) all-reduce(bf16[256]{0:T(256)(128)(2,1)S(1)} %dynamic-slice.1, ...), channel_id=1, replica_groups=mesh['rep'=16,'shard'=8] {'rep'}, use_global_device_ids=true, to_apply=%region_25.0 | all-reduce | flops 1792 | bytes 7168 | tf_op jit(solution)/shard_map/psum | solution.py:272
  1355.5 12.7 fusion.50
  1368.2 19.0 %psum.77 = f32[1,1024]{1,0:T(1,128)S(1)} all-reduce(f32[1,1024]{1,0:T(1,128)S(1)} %fusion.50), channel_id=1, replica_groups=mesh['rep'=16,'shard'=8] {'shard'}, use_global_device_ids=true, to_apply=%region_19.0 | all-reduce | flops 1024 | bytes 8192 | tf_op jit(solution)/shard_map/psum | solution.py:227
  1387.8 30.2 %all-reduce.10.cloned.1.call-done = (bf16[128,3072]{1,0:T(8,128)(2,1)}, bf16[128,1024]{1,0:T(8,128)(2,1)}, bf16[128,4096]{1,0:T(8,128)(2,1)}, bf16[512,1024]{1,0:T(8,128)(2,1)}, bf16[128,6144]{1,0:T(8,128)(2,1)}) async-done(((bf16[128,3072]{1,0:T(8,128)(2,1)}, bf16[128,1024]{1,0:T(8,128)(2,1)}, bf16[128,4096]{1,0:T(8,128)(2,1)}, bf16[512,1024]{1,0:T(8,128)(2,1)}, bf16[128,6144]{1,0:T(8,128)(2,1)}), ...) | async-done | bytes 4718608 | tf_op jit(solution)/shard_map/psum | solution.py:271
  1422.4 2.8 convert_element_type.279
  (152 shorter events, 51.0 us)
Async XLA Ops:
  7.2 150.7 %all-gather.13.cloned.1.call-start = ((), (), s32[]{:S(2)}) async-start(), calls=%async_computation.4 | async-start | bytes 14155776 | tf_op jit(solution)/shard_map/all_gather | solution.py:70
  7.9 239.0 %all-gather.15.cloned.1.call-start = ((), (), s32[]{:S(2)}) async-start(), calls=%async_computation.5 | async-start | bytes 7077888 | tf_op jit(solution)/shard_map/all_gather | solution.py:62
  8.7 295.1 %all-gather.17.cloned.1.call-start = ((), (), s32[]{:S(2)}) async-start(), calls=%async_computation.6 | async-start | bytes 2359296 | tf_op jit(solution)/shard_map/all_gather | solution.py:97
  70.0 176.9 %copy-start.3 = (bf16[1,128,1024]{2,1,0:T(8,128)(2,1)S(1)}, bf16[1,128,1024]{2,1,0:T(8,128)(2,1)}, u32[]{:S(2)}) copy-start(bf16[1,128,1024]{2,1,0:T(8,128)(2,1)} %param.13) | copy-start | bytes 786436
  250.8 3.6 copy-start.25
  250.8 3.7 copy-start.26
  251.6 106.7 %all-gather.19.cloned.1.call-start = ((), (), s32[]{:S(2)}) async-start(), calls=%async_computation.7 | async-start | bytes 2359296 | tf_op jit(solution)/shard_map/all_gather | solution.py:96
  252.5 159.9 %all-gather.21.cloned.1.call-start = ((), (), s32[]{:S(2)}) async-start(), calls=%async_computation.8 | async-start | bytes 2359296 | tf_op jit(solution)/shard_map/all_gather | solution.py:64
  253.0 266.4 %all-gather.23.cloned.1.call-start = ((), (), s32[]{:S(2)}) async-start(), calls=%async_computation.9 | async-start | bytes 9437184 | tf_op jit(solution)/shard_map/all_gather | solution.py:66
  253.6 373.1 %all-gather.25.cloned.1.call-start = ((), (), s32[]{:S(2)}) async-start(), calls=%async_computation.10 | async-start | bytes 9437184 | tf_op jit(solution)/shard_map/all_gather | solution.py:68
  254.4 483.9 %reduce-scatter.15.cloned.1.call-start = ((), (), s32[]{:S(2)}) async-start(), calls=%async_computation.14 | async-start | bytes 2359296
  303.1 58.1 %copy-start.10 = (bf16[1,128,1024]{1,2,0:T(8,128)(2,1)}, bf16[1,128,1024]{1,2,0:T(8,128)(2,1)S(1)}, u32[]{:S(2)}) copy-start(bf16[1,128,1024]{1,2,0:T(8,128)(2,1)S(1)} %copy.41) | copy-start | bytes 786436
  362.6 3.5 copy-start
  362.6 3.5 copy-start.7
  369.0 150.5 %copy-start.23 = (bf16[16,64,128]{2,1,0:T(8,128)(2,1)}, bf16[16,64,128]{2,1,0:T(8,128)(2,1)S(1)}, u32[]{:S(2)}) copy-start(bf16[16,64,128]{2,1,0:T(8,128)(2,1)S(1)} %fusion.16) | copy-start | bytes 786436
  519.5 107.3 %copy-start.16 = (bf16[1,128,1024]{2,1,0:T(8,128)(2,1)S(1)}, bf16[1,128,1024]{2,1,0:T(8,128)(2,1)}, u32[]{:S(2)}) copy-start(bf16[1,128,1024]{2,1,0:T(8,128)(2,1)} %param.15) | copy-start | bytes 786436
  626.8 8.3 copy-start.1
  635.0 3.0 copy-start.8
  635.0 4.1 copy-start.17
  635.0 5.0 copy-start.6
  638.3 0.8 copy-start.13
  639.4 0.7 copy-start.12
  665.3 151.1 %reduce-scatter.13.cloned.1.call-start = ((), (), s32[]{:S(2)}) async-start(), calls=%async_computation.13 | async-start | bytes 2359296
  672.3 6.6 copy-start.11
  676.9 2.0 copy-start.2
  691.9 4.5 copy-start.24
  691.9 4.5 copy-start.27
  696.3 469.9 %reduce-scatter.9.cloned.1.call-start = ((), (), s32[]{:S(2)}) async-start(), calls=%async_computation.11 | async-start | bytes 33030144 | tf_op jit(solution)/shard_map/reduce_scatter | solution.py:236
  722.3 4.1 copy-start.9
  726.4 91.9 %copy-start.20 = (bf16[16,64,128]{2,1,0:T(8,128)(2,1)}, bf16[16,64,128]{2,1,0:T(8,128)(2,1)S(1)}, u32[]{:S(2)}) copy-start(bf16[16,64,128]{2,1,0:T(8,128)(2,1)S(1)} %get-tuple-element.64) | copy-start | bytes 786436
  740.3 78.0 %copy-start.21 = (bf16[1,128,1024]{1,2,0:T(8,128)(2,1)}, bf16[1,128,1024]{1,2,0:T(8,128)(2,1)S(1)}, u32[]{:S(2)}) copy-start(bf16[1,128,1024]{1,2,0:T(8,128)(2,1)S(1)} %copy.48) | copy-start | bytes 786436
  818.3 0.7 copy-start.22
  823.6 8.7 copy-start.4
  823.6 8.7 copy-start.14
  838.5 7.5 copy-start.5
  865.0 1.0 copy-start.18
  865.0 418.1 %reduce-scatter.11.cloned.1.call-start = ((), (), s32[]{:S(2)}) async-start(), calls=%async_computation.12 | async-start | bytes 9437184 | tf_op jit(solution)/shard_map/reduce_scatter | solution.py:243
  871.6 546.4 %all-reduce.10.cloned.1.call-start = ((), (), s32[]{:S(2)}) async-start(), calls=%async_computation.15 | async-start | bytes 9437184 | tf_op jit(solution)/shard_map/psum | solution.py:271
  1172.2 111.0 %copy-start.28 = (u32[128]{0:T(128)S(1)}, u32[128]{0:T(128)}, u32[]{:S(2)}) copy-start(u32[128]{0:T(128)} %constant.43) | copy-start | bytes 1540
  1418.0 7.2 copy-start.19
  1419.8 6.9 copy-start.15
Sparse Core Ops, SparseCore 0:
  10.3 147.5 all-gather.12
  160.2 86.6 all-gather.14
  251.8 51.9 all-gather.16
  306.5 51.7 all-gather.18
  360.5 51.7 all-gather.20
  414.6 104.8 all-gather.22
  521.8 104.8 all-gather.24
  665.4 72.8 reduce-scatter.14
  742.6 73.7 reduce-scatter.12
  865.2 300.9 reduce-scatter.8
  1170.0 113.0 reduce-scatter.10
  1287.3 130.6 all-reduce.9
where the time goes:
time: 1440 us
  waiting for transfers between devices  989 us (69%)
  blocking collectives  210 us (15%)
  matrix products  99.9 us (7%)
  local copies, waits for them, and re-layouts  64.3 us (4%)
  other arithmetic  55 us (4%)
  between operations  17.5 us (1%)
    reduce_scatter x1, waiting for transfers between devices, on_device(): lax.psum_scatter(jnp.concatenate(pieces, axis=1).astype(jnp.bfloat16), 's...  295 us
    reduce_scatter x1, waiting for transfers between devices, on_device(): lax.psum_scatter(jnp.einsum('lrc,lre->ce', active_low, grad_branch_second...  108 us
    all_gather x1, waiting for transfers between devices, on_device(): lax.all_gather(w_fc1, 'shard', axis=0, tiled=True)  104 us
    all_gather x1, waiting for transfers between devices, on_device(): lax.all_gather(w_fc2, 'shard', axis=0, tiled=True)  101 us
    all_gather x1, waiting for transfers between devices, on_device(): lax.all_gather(w_ada, 'shard', axis=0, tiled=True)  87.9 us
    unnamed x14, waiting for transfers between devices  85.5 us
    all_gather x1, waiting for transfers between devices, on_device(): lax.all_gather(w_qkv, 'shard', axis=0, tiled=True)  82.7 us
    all_gather x1, waiting for transfers between devices, on_device(): lax.all_gather(keyset, 'shard', axis=1, tiled=True)  50.6 us
  transfers between devices with their start and end apart: 12, of which 12 were waited for; matrix products, arithmetic and copies ran while one was open for 8% of the time, Pallas kernels for 0%

commit v1 on v0

--- a/solution.py
+++ b/solution.py
@@ -63,7 +63,9 @@
         lax.all_gather(bias_qv, "shard", axis=0, tiled=True),
         lax.all_gather(w_proj, "shard", axis=0, tiled=True),
         lax.all_gather(b_proj, "shard", axis=0, tiled=True),
-        lax.all_gather(w_fc1, "shard", axis=0, tiled=True),
+        jnp.concatenate(
+            lax.all_to_all(jnp.stack([w_fc1] * lax.axis_size("shard")), "shard", 0, 0), axis=0
+        ),
         lax.all_gather(b_fc1, "shard", axis=0, tiled=True),
         lax.all_gather(w_fc2, "shard", axis=0, tiled=True),
         lax.all_gather(b_fc2, "shard", axis=0, tiled=True),

time: 1440 us -> 1530 us (1.062)
  blocking collectives: 210 us -> 300 us
  waiting for transfers between devices: 989 us -> 966 us
    all_gather x1, blocking collectives: 18.8 us -> 109 us  [on_device(): lax.all_gather(b_proj, 'shard', axis=0, tiled=True)]
    unnamed x79 -> x77, local copies, waits for them, and re-layouts: 42 us -> 42.1 us
  transfers between devices with their start and end apart: 12 -> 13, of which waited for: 12 -> 11; matrix products, arithmetic and copies ran while one was open for 8% -> 8% of each run, Pallas kernels for 0% -> 0%
where the time goes in v1:
time: 1530 us; the launch traced here: 1520 us
  waiting for transfers between devices  966 us (63%)
  blocking collectives  300 us (20%)
  matrix products  105 us (7%)
  local copies, waits for them, and re-layouts  68.9 us (5%)
  other arithmetic  54.9 us (4%)
  between operations  17.4 us (1%)
    reduce_scatter x1, waiting for transfers between devices, on_device(): lax.psum_scatter(jnp.concatenate(pieces, axis=1).astype(jnp.bfloat16), 's...  294 us
    all_gather x1, blocking collectives, on_device(): lax.all_gather(b_proj, 'shard', axis=0, tiled=True)  109 us
    reduce_scatter x1, waiting for transfers between devices, on_device(): lax.psum_scatter(jnp.einsum('lrc,lre->ce', active_low, grad_branch_second...  109 us
    all_gather x1, waiting for transfers between devices, on_device(): lax.all_gather(w_fc1, 'shard', axis=0, tiled=True)  98.1 us
    all_gather x1, waiting for transfers between devices, on_device(): lax.all_gather(w_fc2, 'shard', axis=0, tiled=True)  97.9 us
    all_gather x1, waiting for transfers between devices, on_device(): lax.all_gather(w_ada, 'shard', axis=0, tiled=True)  87.9 us
    unnamed x14, waiting for transfers between devices  85.3 us
    all_gather x1, waiting for transfers between devices, on_device(): lax.all_gather(w_qkv, 'shard', axis=0, tiled=True)  82.7 us
  transfers between devices with their start and end apart: 13, of which 11 were waited for; matrix products, arithmetic and copies ran while one was open for 8% of the time, Pallas kernels for 0%

profile of v1, /device:TPU:0, one launch (start us, length us, event | category | flops | bytes accessed | tf_op | source)
XLA Modules:
  0.0 1517.4 jit_solution(3295267185949750497)
XLA Ops:
  9.4 34.7 %all-gather = bf16[8,1,768]{2,1,0:T(2,128)(2,1)S(1)} all-gather(bf16[1,1,768]{2,1,0:T(2,128)(2,1)S(1)} %reshape.417), channel_id=1, replica_groups=mesh['rep'=16,'shard'=8] {'shard'}, dimensions={0}, use_global_device_ids=true | all-gather | bytes 13824 | tf_op jit(solution)/shard_map/all_gather | solution.py:73
  44.7 22.9 %all-gather.1 = bf16[8,1,256]{2,1,0:T(2,128)(2,1)S(1)} all-gather(bf16[1,1,256]{2,1,0:T(2,128)(2,1)S(1)} %reshape.419), channel_id=1, replica_groups=mesh['rep'=16,'shard'=8] {'shard'}, dimensions={0}, use_global_device_ids=true | all-gather | bytes 4608 | tf_op jit(solution)/shard_map/all_gather | solution.py:63
  70.0 87.9 %all-gather.13.cloned.1.call-done = bf16[1024,6144]{1,0:T(8,128)(2,1)} async-done(((bf16[128,6144]{1,0:T(8,128)(2,1)}), bf16[1024,6144]{1,0:T(8,128)(2,1)}) %all-gather.13.cloned.1.call-update) | async-done | bytes 12582928 | tf_op jit(solution)/shard_map/all_gather | solution.py:72
  157.9 6.3 fusion.53
  164.2 82.7 %all-gather.15.cloned.1.call-done = bf16[1024,3072]{1,0:T(8,128)(2,1)} async-done(((bf16[128,3072]{1,0:T(8,128)(2,1)}), bf16[1024,3072]{1,0:T(8,128)(2,1)}) %all-gather.15.cloned.1.call-update) | async-done | bytes 6291472 | tf_op jit(solution)/shard_map/all_gather | solution.py:62
  246.9 3.9 convolution_bitcast_fusion
  254.3 4.5 stack.2
  258.8 5.1 all-to-all-start
  264.0 109.0 %all-gather.2 = bf16[8,1,128]{2,1,0:T(2,128)(2,1)S(1)} all-gather(bf16[1,1,128]{2,1,0:T(2,128)(2,1)S(1)} %bitcast.212), channel_id=1, replica_groups=mesh['rep'=16,'shard'=8] {'shard'}, dimensions={0}, use_global_device_ids=true | all-gather | bytes 2304 | tf_op jit(solution)/shard_map/all_gather | solution.py:65
  373.0 29.7 %all-gather.3 = bf16[8,1,512]{2,1,0:T(2,128)(2,1)S(1)} all-gather(bf16[1,1,512]{2,1,0:T(2,128)(2,1)S(1)} %reshape.423), channel_id=1, replica_groups=mesh['rep'=16,'shard'=8] {'shard'}, dimensions={0}, use_global_device_ids=true | all-gather | bytes 9216 | tf_op jit(solution)/shard_map/all_gather | solution.py:69
  403.0 4.0 copy.40
  407.0 37.6 %all-gather.19.cloned.1.call-done = bf16[1,1024,1024]{2,1,0:T(8,128)(2,1)} async-done(((bf16[1,128,1024]{2,1,0:T(8,128)(2,1)}), bf16[1,1024,1024]{2,1,0:T(8,128)(2,1)}) %all-gather.19.cloned.1.call-update) | async-done | bytes 2097168 | tf_op jit(solution)/shard_map/all_gather | solution.py:98
  444.6 2.9 copy.42
  454.9 43.7 %all-gather.21.cloned.1.call-done = bf16[1024,1024]{1,0:T(8,128)(2,1)} async-done(((bf16[128,1024]{1,0:T(8,128)(2,1)}), bf16[1024,1024]{1,0:T(8,128)(2,1)}) %all-gather.21.cloned.1.call-update) | async-done | bytes 2097168 | tf_op jit(solution)/shard_map/all_gather | solution.py:64
  498.6 2.9 fusion.70
  501.8 6.1 convolution_add_fusion
  507.8 97.9 %all-gather.23.cloned.1.call-done = bf16[4096,1024]{1,0:T(8,128)(2,1)} async-done(((bf16[512,1024]{1,0:T(8,128)(2,1)}), bf16[4096,1024]{1,0:T(8,128)(2,1)}) %all-gather.23.cloned.1.call-update) | async-done | bytes 8388624 | tf_op jit(solution)/shard_map/all_gather | solution.py:70
  605.7 9.2 fusion.74
  614.9 98.1 %all-gather.25.cloned.1.call-done = bf16[1024,4096]{1,0:T(8,128)(2,1)} async-done(((bf16[128,4096]{1,0:T(8,128)(2,1)}), bf16[1024,4096]{1,0:T(8,128)(2,1)}) %all-gather.25.cloned.1.call-update) | async-done | bytes 8388624 | tf_op jit(solution)/shard_map/all_gather | solution.py:133
  713.0 6.9 fusion.33
  725.2 6.7 fusion.13
  731.9 10.8 copy.47
  742.7 4.3 copy.54
  747.3 6.8 multiply_reduce_fusion
  754.2 4.6 multiply_convert_fusion.1
  762.7 10.9 copy.45
  773.6 4.4 copy.55
  778.1 18.8 %all-gather.4 = bf16[8,1,128]{2,1,0:T(2,128)(2,1)S(1)} all-gather(bf16[1,1,128]{2,1,0:T(2,128)(2,1)S(1)} %bitcast.213), channel_id=1, replica_groups=mesh['rep'=16,'shard'=8] {'shard'}, dimensions={0}, use_global_device_ids=true | all-gather | bytes 2304 | tf_op jit(solution)/shard_map/all_gather | solution.py:71
  797.0 3.1 convolution_convert_fusion.3
  800.1 3.9 copy.44
  804.0 4.1 fusion.73
  808.1 5.8 convolution_convert_fusion.1
  813.9 6.0 reduce-scatter.15.cloned.1.call-done
  822.0 76.0 %reduce-scatter.13.cloned.1.call-done = bf16[128,1024]{1,0:T(8,128)(2,1)} async-done(((bf16[1024,1024]{1,0:T(8,128)(2,1)}), bf16[128,1024]{1,0:T(8,128)(2,1)}) %reduce-scatter.13.cloned.1.call-update) | async-done | bytes 262160
  900.8 4.6 convolution_convert_fusion.2
  905.4 6.2 fusion.28
  914.1 6.2 fusion.30
  920.4 7.4 multiply_convert_fusion
  927.8 19.0 %pad_maximum_fusion = bf16[1024,14336]{1,0:T(8,128)(2,1)} fusion(bf16[1024,6144]{1,0:T(8,128)(2,1)} %multiply_convert_fusion, bf16[1024,4096]{1,0:T(8,128)(2,1)} %convolution_convert_fusion.1, bf16[1024,1024]{1,0:T(8,128)(2,1)S(1)} %copy-done.4, bf16[1024,3072]{1,0:T(8,128)(2,1)} %convolution_convert_fusion.2), kind=kLoop, calls=%fused_computation | loop fusion | flops 117440512 | bytes 58720256 | tf_op jit(solution)/shard_map/concatenate | solution.py:239
  947.7 5.7 convolution_convert_fusion
  953.5 294.1 %reduce-scatter.9.cloned.1.call-done = bf16[128,14336]{1,0:T(8,128)(2,1)} async-done(((bf16[1024,14336]{1,0:T(8,128)(2,1)}), bf16[128,14336]{1,0:T(8,128)(2,1)}) %reduce-scatter.9.cloned.1.call-update) | async-done | bytes 3670032 | tf_op jit(solution)/shard_map/reduce_scatter | solution.py:238
  1256.3 108.7 %reduce-scatter.11.cloned.1.call-done = bf16[512,1024]{1,0:T(8,128)(2,1)} async-done(((bf16[4096,1024]{1,0:T(8,128)(2,1)}), bf16[512,1024]{1,0:T(8,128)(2,1)}) %reduce-scatter.11.cloned.1.call-update) | async-done | bytes 1048592 | tf_op jit(solution)/shard_map/reduce_scatter | solution.py:245
  1368.3 37.9 %all-reduce.7 = (bf16[2048]{0:T(1024)(128)(2,1)S(1)}, bf16[1024]{0:T(1024)(128)(2,1)S(1)}, bf16[4096]{0:T(1024)(128)(2,1)S(1)}, bf16[1024]{0:T(1024)(128)(2,1)S(1)}, bf16[6144]{0:T(1024)(128)(2,1)S(1)}) all-reduce(bf16[2048]{0:T(1024)(128)(2,1)S(1)} %pad_maximum_fusion.1, ...), channel_id=5, replica_groups=mesh['rep'=16,'shard'=8] {'shard'}, use_global_device_ids=true, to_apply=%region_24.0.clone | all-reduce | flops 14336 | bytes 57344
  1406.6 27.9 %all-reduce.5 = (bf16[256]{0:T(256)(128)(2,1)S(1)}, bf16[128]{0:T(256)(128)(2,1)S(1)}, bf16[512]{0:T(512)(128)(2,1)S(1)}, bf16[128]{0:T(256)(128)(2,1)S(1)}, bf16[768]{0:T(1024)(128)(2,1)S(1)}) all-reduce(bf16[256]{0:T(256)(128)(2,1)S(1)} %dynamic-slice.1, ...), channel_id=1, replica_groups=mesh['rep'=16,'shard'=8] {'rep'}, use_global_device_ids=true, to_apply=%region_25.0 | all-reduce | flops 1792 | bytes 7168 | tf_op jit(solution)/shard_map/psum | solution.py:274
  1437.3 12.7 fusion.50
  1450.0 19.0 %psum.77 = f32[1,1024]{1,0:T(1,128)S(1)} all-reduce(f32[1,1024]{1,0:T(1,128)S(1)} %fusion.50), channel_id=1, replica_groups=mesh['rep'=16,'shard'=8] {'shard'}, use_global_device_ids=true, to_apply=%region_19.0 | all-reduce | flops 1024 | bytes 8192 | tf_op jit(solution)/shard_map/psum | solution.py:229
  1469.6 30.1 %all-reduce.10.cloned.1.call-done = (bf16[128,3072]{1,0:T(8,128)(2,1)}, bf16[128,1024]{1,0:T(8,128)(2,1)}, bf16[128,4096]{1,0:T(8,128)(2,1)}, bf16[512,1024]{1,0:T(8,128)(2,1)}, bf16[128,6144]{1,0:T(8,128)(2,1)}) async-done(((bf16[128,3072]{1,0:T(8,128)(2,1)}, bf16[128,1024]{1,0:T(8,128)(2,1)}, bf16[128,4096]{1,0:T(8,128)(2,1)}, bf16[512,1024]{1,0:T(8,128)(2,1)}, bf16[128,6144]{1,0:T(8,128)(2,1)}), ...) | async-done | bytes 4718608 | tf_op jit(solution)/shard_map/psum | solution.py:273
  1504.1 2.8 convert_element_type.279
  (153 shorter events, 55.7 us)
Async XLA Ops:
  7.2 150.7 %all-gather.13.cloned.1.call-start = ((), (), s32[]{:S(2)}) async-start(), calls=%async_computation.5 | async-start | bytes 14155776 | tf_op jit(solution)/shard_map/all_gather | solution.py:72
  7.9 239.0 %all-gather.15.cloned.1.call-start = ((), (), s32[]{:S(2)}) async-start(), calls=%async_computation.6 | async-start | bytes 7077888 | tf_op jit(solution)/shard_map/all_gather | solution.py:62
  8.7 394.3 %all-gather.17.cloned.1.call-start = ((), (), s32[]{:S(2)}) async-start(), calls=%async_computation.7 | async-start | bytes 2359296 | tf_op jit(solution)/shard_map/all_gather | solution.py:99
  70.0 176.9 %copy-start.2 = (bf16[1,128,1024]{2,1,0:T(8,128)(2,1)S(1)}, bf16[1,128,1024]{2,1,0:T(8,128)(2,1)}, u32[]{:S(2)}) copy-start(bf16[1,128,1024]{2,1,0:T(8,128)(2,1)} %param.13) | copy-start | bytes 786436
  250.8 3.6 copy-start.8
  251.6 193.0 %all-gather.19.cloned.1.call-start = ((), (), s32[]{:S(2)}) async-start(), calls=%async_computation.8 | async-start | bytes 2359296 | tf_op jit(solution)/shard_map/all_gather | solution.py:98
  252.4 246.2 %all-gather.21.cloned.1.call-start = ((), (), s32[]{:S(2)}) async-start(), calls=%async_computation.9 | async-start | bytes 2359296 | tf_op jit(solution)/shard_map/all_gather | solution.py:64
  253.0 352.7 %all-gather.23.cloned.1.call-start = ((), (), s32[]{:S(2)}) async-start(), calls=%async_computation.10 | async-start | bytes 9437184 | tf_op jit(solution)/shard_map/all_gather | solution.py:70
  253.6 459.4 %all-gather.25.cloned.1.call-start = ((), (), s32[]{:S(2)}) async-start(), calls=%async_computation.11 | async-start | bytes 9437184 | tf_op jit(solution)/shard_map/all_gather | solution.py:133
  258.8 5.2 copy-start.25
  258.8 114.2 %copy-start.24 = (bf16[512]{0:T(512)(128)(2,1)S(1)}, bf16[512]{0:T(512)(128)(2,1)}, u32[]{:S(2)}) copy-start(bf16[512]{0:T(512)(128)(2,1)} %param.21) | copy-start | bytes 3076
  258.8 242.9 %all-to-all-start = ((bf16[8,128,4096]{2,1,0:T(8,128)(2,1)}), bf16[8,128,4096]{2,1,0:T(8,128)(2,1)}, u32[]{:S(2)}, u32[]{:S(2)}) async-start(bf16[8,128,4096]{2,1,0:T(8,128)(2,1)} %stack.2), calls=%async_computation | async-start | bytes 16777216 | tf_op jit(solution)/shard_map/all_to_all | solution.py:67
  263.9 556.1 %reduce-scatter.15.cloned.1.call-start = ((), (), s32[]{:S(2)}) async-start(), calls=%async_computation.15 | async-start | bytes 2359296
  402.9 44.5 %copy-start.9 = (bf16[1,128,1024]{1,2,0:T(8,128)(2,1)}, bf16[1,128,1024]{1,2,0:T(8,128)(2,1)S(1)}, u32[]{:S(2)}) copy-start(bf16[1,128,1024]{1,2,0:T(8,128)(2,1)S(1)} %copy.41) | copy-start | bytes 786436
  448.9 3.5 copy-start
  448.9 3.5 copy-start.6
  454.9 46.8 %copy-start.22 = (bf16[16,64,128]{2,1,0:T(8,128)(2,1)}, bf16[16,64,128]{2,1,0:T(8,128)(2,1)S(1)}, u32[]{:S(2)}) copy-start(bf16[16,64,128]{2,1,0:T(8,128)(2,1)S(1)} %fusion.16) | copy-start | bytes 786436
  501.7 104.0 %copy-start.15 = (bf16[1,128,1024]{2,1,0:T(8,128)(2,1)S(1)}, bf16[1,128,1024]{2,1,0:T(8,128)(2,1)}, u32[]{:S(2)}) copy-start(bf16[1,128,1024]{2,1,0:T(8,128)(2,1)} %param.15) | copy-start | bytes 786436
  713.0 8.0 copy-start.16
  713.0 8.9 copy-start.5
  720.2 0.8 copy-start.12
  721.2 0.7 copy-start.11
  747.1 151.0 %reduce-scatter.13.cloned.1.call-start = ((), (), s32[]{:S(2)}) async-start(), calls=%async_computation.14 | async-start | bytes 2359296
  754.2 6.5 copy-start.10
  758.7 1.9 copy-start.1
  773.6 4.5 copy-start.26
  773.6 23.2 %copy-start.23 = (bf16[1,1024]{1,0:T(2,128)(2,1)S(1)}, bf16[1,1024]{1,0:T(2,128)(2,1)}, u32[]{:S(2)}) copy-start(bf16[1,1024]{1,0:T(2,128)(2,1)} %param.14) | copy-start | bytes 6148
  778.0 469.5 %reduce-scatter.9.cloned.1.call-start = ((), (), s32[]{:S(2)}) async-start(), calls=%async_computation.12 | async-start | bytes 33030144 | tf_op jit(solution)/shard_map/reduce_scatter | solution.py:238
  804.0 4.1 copy-start.7
  808.1 92.0 %copy-start.19 = (bf16[16,64,128]{2,1,0:T(8,128)(2,1)}, bf16[16,64,128]{2,1,0:T(8,128)(2,1)S(1)}, u32[]{:S(2)}) copy-start(bf16[16,64,128]{2,1,0:T(8,128)(2,1)S(1)} %get-tuple-element.64) | copy-start | bytes 786436
  822.0 78.1 %copy-start.20 = (bf16[1,128,1024]{1,2,0:T(8,128)(2,1)}, bf16[1,128,1024]{1,2,0:T(8,128)(2,1)S(1)}, u32[]{:S(2)}) copy-start(bf16[1,128,1024]{1,2,0:T(8,128)(2,1)S(1)} %copy.48) | copy-start | bytes 786436
  900.1 0.7 copy-start.21
  905.4 8.7 copy-start.3
  905.4 8.7 copy-start.13
  920.3 7.5 copy-start.4
  946.8 1.0 copy-start.17
  946.8 418.1 %reduce-scatter.11.cloned.1.call-start = ((), (), s32[]{:S(2)}) async-start(), calls=%async_computation.13 | async-start | bytes 9437184 | tf_op jit(solution)/shard_map/reduce_scatter | solution.py:245
  953.4 546.3 %all-reduce.10.cloned.1.call-start = ((), (), s32[]{:S(2)}) async-start(), calls=%async_computation.16 | async-start | bytes 9437184 | tf_op jit(solution)/shard_map/psum | solution.py:273
  1253.5 111.4 %copy-start.27 = (u32[128]{0:T(128)S(1)}, u32[128]{0:T(128)}, u32[]{:S(2)}) copy-start(u32[128]{0:T(128)} %constant.43) | copy-start | bytes 1540
  1499.7 7.1 copy-start.18
  1499.7 8.7 copy-start.14
Sparse Core Ops, SparseCore 0:
  10.3 147.4 all-gather.12
  160.2 86.6 all-gather.14
  251.7 138.2 all-gather.16
  392.8 51.7 all-gather.18
  446.8 51.7 all-gather.20
  500.8 104.8 all-gather.22
  608.1 104.8 all-gather.24
  747.2 72.7 reduce-scatter.14
  824.3 73.7 reduce-scatter.12
  946.9 300.5 reduce-scatter.8
  1251.3 113.5 reduce-scatter.10
  1369.1 130.5 all-reduce.9
